TPU v7x, 256 devices: a whole 4x4x8 slice. The times are simulated.
256 devices in a mesh: face: 128 (over x, y_hi, z, core), sub: 2 (over y_lo).
Axes of the slice: x: 4, y: 4 (y_hi: 2, y_lo: 2; y = y_hi * 2 + y_lo), z: 8, core: 2. Of those that a mesh axis runs over, the one named last changes fastest.
Arguments:
- inputs: bfloat16 [128, 2, 64, 64, 128], P('face', 'sub'), may hold values from -6 to 6
- kernel_one: bfloat16 [3, 3, 128, 128], replicated, may hold values from -0.1875 to 0.1875
- kernel_two: bfloat16 [3, 3, 128, 128], replicated, may hold values from -0.1875 to 0.1875
- cotangent: bfloat16 [128, 2, 64, 64, 128], P('face', 'sub'), may hold values from -6 to 6
- edge_codes: int32 [128, 2, 4], replicated, may hold values from 0 to 7
- corner_codes: int32 [128, 2, 4], replicated, may hold values from 0 to 3
Outputs:
- outputs: bfloat16 [128, 2, 64, 64, 128], P('face', 'sub')
- grad_inputs: bfloat16 [128, 2, 64, 64, 128], P('face', 'sub')
- grad_kernel_one: float32 [3, 3, 128, 128], replicated
- grad_kernel_two: float32 [3, 3, 128, 128], replicated
All inputs are finite; a program needn't handle non-finite values.
Results may differ from a plain program's by a relative error of at most 0.005.
Values may be sent and summed in bfloat16 or wider, within the bound.
No kernel may reach another device: no remote copies, remote signals or barrier semaphores. Data moves between devices by JAX's collectives and lax.ppermute only.
A program may use at most 128 MiB of HBM per device.

v0:
```python
import math
import jax
import jax.numpy as jnp
from jax import lax
from jax.sharding import PartitionSpec as P

GRID_ROWS = 8


def shifted(x, axis, by):
    size = lax.axis_size(axis)
    return lax.ppermute(x, axis, [(i, (i + by) % size) for i in range(size)])


def neighbour_steps():
    row_width = lax.axis_size("face") // GRID_ROWS * lax.axis_size("sub")
    return (
        [-row_width, 1, row_width, -1],
        [-row_width - 1, -row_width + 1, row_width + 1, row_width - 1],
    )


def pull_sets(payload, offset):
    return shifted(payload, ("face", "sub"), offset)


def back_sets(payload, offset):
    return shifted(payload, ("face", "sub"), offset)


def fill_halo(fields, edge_codes, corner_codes):
    device_count = lax.axis_size(("face", "sub"))
    own_index = lax.axis_index(("face", "sub"))
    side_len = fields.shape[1]
    edge_table = edge_codes.reshape(device_count, 4)
    corner_table = corner_codes.reshape(device_count, 4)
    edge_steps, corner_steps = neighbour_steps()
    edge_sets = jnp.stack([fields[0, 0], fields[0, :, -1], fields[0, -1], fields[0, :, 0]])
    corner_sets = jnp.stack(
        [fields[0, 0, 0], fields[0, 0, -1], fields[0, -1, -1], fields[0, -1, 0]]
    )
    strips = []
    corner_vals = []
    for direction in range(4):
        arrived = pull_sets(edge_sets, -edge_steps[direction])
        edge_code = edge_table[own_index, direction]
        picked = lax.dynamic_index_in_dim(arrived, edge_code % 4, 0, keepdims=False)
        strips.append(jnp.where(edge_code >= 4, picked[::-1], picked))
    for corner in range(4):
        arrived = pull_sets(corner_sets, -corner_steps[corner])
        corner_vals.append(
            lax.dynamic_index_in_dim(arrived, corner_table[own_index, corner], 0, keepdims=False)
        )
    padded = jnp.pad(fields, ((0, 0), (1, 1), (1, 1), (0, 0)))
    last = side_len + 1
    padded = padded.at[0, 0, 1:last].set(strips[0]).at[0, 1:last, last].set(strips[1])
    padded = padded.at[0, last, 1:last].set(strips[2]).at[0, 1:last, 0].set(strips[3])
    padded = padded.at[0, 0, 0].set(corner_vals[0]).at[0, 0, last].set(corner_vals[1])
    padded = padded.at[0, last, last].set(corner_vals[2]).at[0, last, 0].set(corner_vals[3])
    return padded


def return_halo(grad_pad, edge_codes, corner_codes):
    device_count = lax.axis_size(("face", "sub"))
    own_index = lax.axis_index(("face", "sub"))
    edge_table = edge_codes.reshape(device_count, 4)
    corner_table = corner_codes.reshape(device_count, 4)
    edge_steps, corner_steps = neighbour_steps()
    interior = grad_pad[:, 1:-1, 1:-1]
    pad_strips = [
        grad_pad[0, 0, 1:-1],
        grad_pad[0, 1:-1, -1],
        grad_pad[0, -1, 1:-1],
        grad_pad[0, 1:-1, 0],
    ]
    pad_cells = [grad_pad[0, 0, 0], grad_pad[0, 0, -1], grad_pad[0, -1, -1], grad_pad[0, -1, 0]]
    slot_ids = jnp.arange(4, dtype=jnp.int32)
    edge_add = jnp.zeros((4,) + pad_strips[0].shape, jnp.float32)
    corner_add = jnp.zeros((4,) + pad_cells[0].shape, jnp.float32)
    for direction in range(4):
        edge_code = edge_table[own_index, direction]
        returned = jnp.where(edge_code >= 4, pad_strips[direction][::-1], pad_strips[direction])
        slots = (slot_ids == edge_code % 4).astype(jnp.float32)
        edge_add = edge_add + back_sets(
            slots[:, None, None] * returned[None], edge_steps[direction]
        )
    for corner in range(4):
        slots = (slot_ids == corner_table[own_index, corner]).astype(jnp.float32)
        corner_add = corner_add + back_sets(
            slots[:, None] * pad_cells[corner][None], corner_steps[corner]
        )
    interior = interior.at[0, 0, :].add(edge_add[0]).at[0, :, -1].add(edge_add[1])
    interior = interior.at[0, -1, :].add(edge_add[2]).at[0, :, 0].add(edge_add[3])
    interior = interior.at[0, 0, 0].add(corner_add[0]).at[0, 0, -1].add(corner_add[1])
    interior = interior.at[0, -1, -1].add(corner_add[2]).at[0, -1, 0].add(corner_add[3])
    return interior


def conv_forward(padded, kernel):
    return lax.conv_general_dilated(
        padded,
        kernel,
        (1, 1),
        "VALID",
        dimension_numbers=("NHWC", "HWIO", "NHWC"),
        preferred_element_type=jnp.float32,
    )


def conv_inputs(upstream, kernel):
    widened = jnp.pad(upstream, ((0, 0), (2, 2), (2, 2), (0, 0)))
    turned = jnp.transpose(jnp.flip(kernel, (0, 1)), (0, 1, 3, 2))
    return lax.conv_general_dilated(
        widened,
        turned,
        (1, 1),
        "VALID",
        dimension_numbers=("NHWC", "HWIO", "NHWC"),
        preferred_element_type=jnp.float32,
    )


def conv_kernel(padded, upstream):
    side_len = upstream.shape[1]
    chans = upstream.shape[-1]
    flat_up = upstream.reshape(-1, chans)
    rows_out = []
    for row_off in range(3):
        cols_out = []
        for col_off in range(3):
            window = padded[
                :, row_off : row_off + side_len, col_off : col_off + side_len, :
            ].reshape(-1, chans)
            cols_out.append(
                lax.dot_general(
                    window, flat_up, (((0,), (0,)), ((), ())), preferred_element_type=jnp.float32
                )
            )
        rows_out.append(jnp.stack(cols_out))
    return jnp.stack(rows_out)


def local(inputs, kernel_one, kernel_two, cotangent, edge_codes, corner_codes):
    fields = inputs[0]
    upstream = cotangent[0]
    side_len = fields.shape[1]
    norm_factor = 1.0 / math.sqrt(lax.axis_size(("face", "sub")) * side_len * side_len)
    padded_one = fill_halo(fields, edge_codes, corner_codes)
    preact = conv_forward(padded_one, kernel_one)
    hidden = jax.nn.silu(preact).astype(jnp.bfloat16)
    padded_two = fill_halo(hidden, edge_codes, corner_codes)
    outputs = conv_forward(padded_two, kernel_two).astype(jnp.bfloat16)
    grad_two = conv_kernel(padded_two, upstream)
    grad_hidden = return_halo(conv_inputs(upstream, kernel_two), edge_codes, corner_codes)
    sigmoid_vals = jax.nn.sigmoid(preact)
    grad_pre = (grad_hidden * sigmoid_vals * (1.0 + preact * (1.0 - sigmoid_vals))).astype(
        jnp.bfloat16
    )
    grad_one = conv_kernel(padded_one, grad_pre)
    grad_fields = return_halo(conv_inputs(grad_pre, kernel_one), edge_codes, corner_codes).astype(
        jnp.bfloat16
    )
    grad_one, grad_two = lax.psum((grad_one, grad_two), ("face", "sub"))
    return (outputs[None], grad_fields[None], grad_one * norm_factor, grad_two * norm_factor)


def solution(mesh):
    in_specs = (
        P("face", "sub", None, None, None),
        P(),
        P(),
        P("face", "sub", None, None, None),
        P(),
        P(),
    )
    out_specs = (P("face", "sub", None, None, None), P("face", "sub", None, None, None), P(), P())
    return jax.shard_map(local, mesh=mesh, in_specs=in_specs, out_specs=out_specs, check_vma=False)
```

profile of v0, /device:TPU:8, one launch (start us, length us, event | category | flops | bytes accessed | tf_op | source)
XLA Modules:
  0.0 517.0 jit_solution(1585408178761811315)
XLA Ops:
  8.0 3.3 collective-permute-start.7
  12.3 5.7 %collective-permute-start.5 = (bf16[4,128]{1,0:T(4,128)(2,1)S(1)}, bf16[4,128]{1,0:T(4,128)(2,1)S(1)}, u32[]{:S(2)}, u32[]{:S(2)}) collective-permute-start(bf16[4,128]{1,0:T(4,128)(2,1)S(1)} %pad_maximum_fusion.4), channel_id=1, source_target_pairs={{0,31},{1,32},{2,33},{3,34},{4,35},{5,36},{6,37},{7,38},{8,39},{9,... | collective-permute-start | bytes 3080 | tf_op jit(solution)/shard_map/ppermute | solution.py:12
  33.0 1.9 copy.179
  35.9 3.1 convolution_select_fusion.1
  44.6 2.0 and_reduce_fusion
  51.7 1.7 slice.1266
  53.4 1.5 pad.122
  57.4 4.2 collective-permute-start.20
  61.8 4.5 collective-permute-start.23
  66.4 3.7 collective-permute-start.2
  70.1 4.6 collective-permute-start.1
  75.1 4.6 collective-permute-start.19
  80.3 2.3 collective-permute-done
  82.7 5.7 %collective-permute-start.16 = (f32[4,64,128]{2,1,0:T(8,128)S(1)}, f32[4,64,128]{2,1,0:T(8,128)S(1)}, u32[]{:S(2)}, u32[]{:S(2)}) collective-permute-start(f32[4,64,128]{2,1,0:T(8,128)S(1)} %broadcast_multiply_fusion.9), channel_id=1, source_target_pairs={{0,224},{1,225},{2,226},{3,227},{4,228},{5,229},{6,230},{7,231},{8... | collective-permute-start | bytes 393224 | tf_op jit(solution)/shard_map/ppermute | solution.py:12
  90.0 1.4 scatter.54
  91.3 1.7 scatter.55
  93.0 1.4 scatter.56
  94.4 1.7 scatter.59
  97.3 1.3 scatter.61
  99.7 1.3 scatter.65
  101.0 1.4 copy.155
  103.2 5.0 add_divide_fusion
  111.0 1.8 copy.116
  113.3 1.9 copy.117
  115.2 2.2 collective-permute-start.14
  118.9 3.8 collective-permute-start.13
  122.8 1.5 collective-permute-done.13
  124.5 7.6 %collective-permute-done.12 = bf16[4,128]{1,0:T(4,128)(2,1)S(1)} collective-permute-done((bf16[4,128]{1,0:T(4,128)(2,1)}, bf16[4,128]{1,0:T(4,128)(2,1)S(1)}, u32[]{:S(2)}, u32[]{:S(2)}) %collective-permute-start.12) | collective-permute-done | bytes 1056 | tf_op jit(solution)/shard_map/ppermute | solution.py:12
  132.1 1.7 collective-permute-start.11
  133.9 1.7 collective-permute-start.10
  135.6 3.8 collective-permute-start.9
  139.4 3.0 collective-permute-start.8
  143.5 1.8 scatter-add.54
  145.2 2.6 fusion.45
  147.9 2.2 broadcast_select_fusion.1
  150.1 2.4 scatter-add.56
  161.0 3.7 fusion.5
  164.7 2.0 convolution_bitcast_fusion.16
  166.6 2.0 convolution_bitcast_fusion.15
  168.6 1.9 convolution_bitcast_fusion.14
  170.5 2.0 convolution_bitcast_fusion.13
  172.5 2.0 convolution_bitcast_fusion.12
  174.5 1.9 convolution_bitcast_fusion.11
  176.4 2.0 convolution_bitcast_fusion.10
  178.4 2.0 convolution_bitcast_fusion.9
  180.4 2.3 convolution_bitcast_fusion.17
  183.7 3.1 convolution_select_fusion
  188.1 1.3 copy-done.4
  190.2 3.3 slice.1289
  194.8 3.9 fusion.71
  199.8 2.9 select_convert_fusion
  203.1 1.6 copy.147
  205.1 4.8 collective-permute-start.31
  209.9 4.1 collective-permute-start.28
  216.3 2.9 copy.152
  221.6 4.6 collective-permute-start.26
  243.2 1.4 collective-permute-start.24
  244.6 6.0 %collective-permute-start.27 = (f32[4,64,128]{2,1,0:T(8,128)S(1)}, f32[4,64,128]{2,1,0:T(8,128)S(1)}, u32[]{:S(2)}, u32[]{:S(2)}) collective-permute-start(f32[4,64,128]{2,1,0:T(8,128)S(1)} %copy-done.18), channel_id=1, source_target_pairs={{0,255},{1,0},{2,1},{3,2},{4,3},{5,4},{6,5},{7,6},{8,7},{9,8},{10,... | collective-permute-start | bytes 393224 | tf_op jit(solution)/shard_map/ppermute | solution.py:12
  250.7 2.5 collective-permute-done.27
  253.1 2.5 collective-permute-done.25
  260.5 1.6 copy.148
  262.2 243.9 %all-reduce.5.cloned.1.call-done = (f32[3,3,128,128]{3,2,1,0:T(8,128)}, f32[3,3,128,128]{3,2,1,0:T(8,128)}) async-done(((f32[3,3,128,128]{3,2,1,0:T(8,128)}, f32[3,3,128,128]{3,2,1,0:T(8,128)}), (f32[3,3,128,128]{3,2,1,0:T(8,128)}, f32[3,3,128,128]{3,2,1,0:T(8,128)})) %all-reduce.5.cloned.1.call-update) | async-done | bytes 1179664 | tf_op jit(solution)/shard_map/psum | solution.py:163
  506.0 1.9 broadcast_multiply_fusion.1
  508.0 1.9 broadcast_multiply_fusion
  (330 shorter events, 65.4 us)
Async XLA Ops:
  7.2 95.6 %copy-start = (bf16[3,3,128,128]{3,2,1,0:T(8,128)(2,1)S(1)}, bf16[3,3,128,128]{3,2,1,0:T(8,128)(2,1)}, u32[]{:S(2)}) copy-start(bf16[3,3,128,128]{3,2,1,0:T(8,128)(2,1)} %param.71) | copy-start | bytes 884740
  7.2 498.9 %all-reduce.5.cloned.1.call-start = ((), (), s32[]{:S(2)}) async-start(), calls=%async_computation | async-start | bytes 2359296 | tf_op jit(solution)/shard_map/psum | solution.py:163
  8.0 49.4 %collective-permute-start.7 = (bf16[4,128]{1,0:T(4,128)(2,1)S(1)}, bf16[4,128]{1,0:T(4,128)(2,1)S(1)}, u32[]{:S(2)}, u32[]{:S(2)}) collective-permute-start(bf16[4,128]{1,0:T(4,128)(2,1)S(1)} %pad_maximum_fusion.4), channel_id=1, source_target_pairs={{0,225},{1,226},{2,227},{3,228},{4,229},{5,230},{6,231},{7,232},{8... | collective-permute-start | bytes 3080 | tf_op jit(solution)/shard_map/ppermute | solution.py:12
  11.3 50.3 %collective-permute-start.6 = (bf16[4,128]{1,0:T(4,128)(2,1)S(1)}, bf16[4,128]{1,0:T(4,128)(2,1)S(1)}, u32[]{:S(2)}, u32[]{:S(2)}) collective-permute-start(bf16[4,128]{1,0:T(4,128)(2,1)S(1)} %pad_maximum_fusion.4), channel_id=1, source_target_pairs={{0,223},{1,224},{2,225},{3,226},{4,227},{5,228},{6,229},{7,230},{8... | collective-permute-start | bytes 3080 | tf_op jit(solution)/shard_map/ppermute | solution.py:12
  12.3 49.4 %collective-permute-start.5 = (bf16[4,128]{1,0:T(4,128)(2,1)S(1)}, bf16[4,128]{1,0:T(4,128)(2,1)S(1)}, u32[]{:S(2)}, u32[]{:S(2)}) collective-permute-start(bf16[4,128]{1,0:T(4,128)(2,1)S(1)} %pad_maximum_fusion.4), channel_id=1, source_target_pairs={{0,31},{1,32},{2,33},{3,34},{4,35},{5,36},{6,37},{7,38},{8,39},{9,... | collective-permute-start | bytes 3080 | tf_op jit(solution)/shard_map/ppermute | solution.py:12
  18.0 48.3 %collective-permute-start.4 = (bf16[4,128]{1,0:T(4,128)(2,1)S(1)}, bf16[4,128]{1,0:T(4,128)(2,1)S(1)}, u32[]{:S(2)}, u32[]{:S(2)}) collective-permute-start(bf16[4,128]{1,0:T(4,128)(2,1)S(1)} %pad_maximum_fusion.4), channel_id=1, source_target_pairs={{0,33},{1,34},{2,35},{3,36},{4,37},{5,38},{6,39},{7,40},{8,41},{9,... | collective-permute-start | bytes 3080 | tf_op jit(solution)/shard_map/ppermute | solution.py:12
  19.8 68.6 %collective-permute-start.3 = (bf16[4,64,128]{2,1,0:T(8,128)(2,1)S(1)}, bf16[4,64,128]{2,1,0:T(8,128)(2,1)}, u32[]{:S(2)}, u32[]{:S(2)}) collective-permute-start(bf16[4,64,128]{2,1,0:T(8,128)(2,1)S(1)} %pad_maximum_fusion.2), channel_id=1, source_target_pairs={{0,1},{1,2},{2,3},{3,4},{4,5},{5,6},{6,7},{7,8},{8,9},{9,10},{10,1... | collective-permute-start | bytes 196616 | tf_op jit(solution)/shard_map/ppermute | solution.py:12
  39.6 5.0 copy-start.40
  39.6 5.0 copy-start.41
  39.8 13.6 %copy-start.3 = (f32[1,66,66,128]{3,1,2,0:T(8,128)}, f32[1,66,66,128]{3,1,2,0:T(8,128)S(1)}, u32[]{:S(2)}) copy-start(f32[1,66,66,128]{3,1,2,0:T(8,128)S(1)} %slice_bitcast_fusion) | copy-start | bytes 6690820
  41.3 2.2 copy-start.32
  41.3 12.1 %copy-start.29 = (f32[4]{0:T(128)}, f32[4]{0:T(128)S(1)}, u32[]{:S(2)}) copy-start(f32[4]{0:T(128)S(1)} %compare_convert_fusion.7) | copy-start | bytes 52
  42.0 1.5 copy-start.34
  43.2 10.2 %copy-start.36 = (f32[4]{0:T(128)}, f32[4]{0:T(128)S(1)}, u32[]{:S(2)}) copy-start(f32[4]{0:T(128)S(1)} %compare_convert_fusion.3) | copy-start | bytes 52
  51.7 1.7 copy-start.16
  57.4 9.0 %collective-permute-start.20 = (f32[4,128]{1,0:T(4,128)S(1)}, f32[4,128]{1,0:T(4,128)S(1)}, u32[]{:S(2)}, u32[]{:S(2)}) collective-permute-start(f32[4,128]{1,0:T(4,128)S(1)} %broadcast_multiply_fusion.17), channel_id=1, source_target_pairs={{0,223},{1,224},{2,225},{3,226},{4,227},{5,228},{6,229},{7,230},{8... | collective-permute-start | bytes 6152 | tf_op jit(solution)/shard_map/ppermute | solution.py:12
  61.6 8.4 %collective-permute-start.22 = (f32[4,128]{1,0:T(4,128)S(1)}, f32[4,128]{1,0:T(4,128)S(1)}, u32[]{:S(2)}, u32[]{:S(2)}) collective-permute-start(f32[4,128]{1,0:T(4,128)S(1)} %broadcast_multiply_fusion.15), channel_id=1, source_target_pairs={{0,33},{1,34},{2,35},{3,36},{4,37},{5,38},{6,39},{7,40},{8,41},{9,... | collective-permute-start | bytes 6152 | tf_op jit(solution)/shard_map/ppermute | solution.py:12
  61.8 12.9 %collective-permute-start.23 = (f32[4,128]{1,0:T(4,128)S(1)}, f32[4,128]{1,0:T(4,128)S(1)}, u32[]{:S(2)}, u32[]{:S(2)}) collective-permute-start(f32[4,128]{1,0:T(4,128)S(1)} %broadcast_multiply_fusion.14), channel_id=1, source_target_pairs={{0,31},{1,32},{2,33},{3,34},{4,35},{5,36},{6,37},{7,38},{8,39},{9,... | collective-permute-start | bytes 6152 | tf_op jit(solution)/shard_map/ppermute | solution.py:12
  66.3 8.8 %collective-permute-start.21 = (f32[4,128]{1,0:T(4,128)S(1)}, f32[4,128]{1,0:T(4,128)S(1)}, u32[]{:S(2)}, u32[]{:S(2)}) collective-permute-start(f32[4,128]{1,0:T(4,128)S(1)} %broadcast_multiply_fusion.16), channel_id=1, source_target_pairs={{0,225},{1,226},{2,227},{3,228},{4,229},{5,230},{6,231},{7,232},{8... | collective-permute-start | bytes 6152 | tf_op jit(solution)/shard_map/ppermute | solution.py:12
  66.4 16.3 %collective-permute-start.2 = (bf16[4,64,128]{2,1,0:T(8,128)(2,1)S(1)}, bf16[4,64,128]{2,1,0:T(8,128)(2,1)S(1)}, u32[]{:S(2)}, u32[]{:S(2)}) collective-permute-start(bf16[4,64,128]{2,1,0:T(8,128)(2,1)S(1)} %pad_maximum_fusion.2), channel_id=1, source_target_pairs={{0,224},{1,225},{2,226},{3,227},{4,228},{5,229},{6,230},{7,231},{8... | collective-permute-start | bytes 196616 | tf_op jit(solution)/shard_map/ppermute | solution.py:12
  70.1 10.2 %collective-permute-start.1 = (bf16[4,64,128]{2,1,0:T(8,128)(2,1)S(1)}, bf16[4,64,128]{2,1,0:T(8,128)(2,1)S(1)}, u32[]{:S(2)}, u32[]{:S(2)}) collective-permute-start(bf16[4,64,128]{2,1,0:T(8,128)(2,1)S(1)} %pad_maximum_fusion.2), channel_id=1, source_target_pairs={{0,255},{1,0},{2,1},{3,2},{4,3},{5,4},{6,5},{7,6},{8,7},{9,8},{10,... | collective-permute-start | bytes 196616 | tf_op jit(solution)/shard_map/ppermute | solution.py:12
  74.6 8.0 %collective-permute-start = (bf16[4,64,128]{2,1,0:T(8,128)(2,1)S(1)}, bf16[4,64,128]{2,1,0:T(8,128)(2,1)S(1)}, u32[]{:S(2)}, u32[]{:S(2)}) collective-permute-start(bf16[4,64,128]{2,1,0:T(8,128)(2,1)S(1)} %pad_maximum_fusion.2), channel_id=1, source_target_pairs={{0,32},{1,33},{2,34},{3,35},{4,36},{5,37},{6,38},{7,39},{8,40},{9,... | collective-permute-start | bytes 196616 | tf_op jit(solution)/shard_map/ppermute | solution.py:12
  75.1 58.8 %collective-permute-start.19 = (f32[4,64,128]{2,1,0:T(8,128)}, f32[4,64,128]{2,1,0:T(8,128)S(1)}, u32[]{:S(2)}, u32[]{:S(2)}) collective-permute-start(f32[4,64,128]{2,1,0:T(8,128)} %broadcast_multiply_fusion.6), channel_id=1, source_target_pairs={{0,255},{1,0},{2,1},{3,2},{4,3},{5,4},{6,5},{7,6},{8,7},{9,8},{10,... | collective-permute-start | bytes 393224 | tf_op jit(solution)/shard_map/ppermute | solution.py:12
  80.2 55.4 %collective-permute-start.17 = (f32[4,64,128]{2,1,0:T(8,128)S(1)}, f32[4,64,128]{2,1,0:T(8,128)S(1)}, u32[]{:S(2)}, u32[]{:S(2)}) collective-permute-start(f32[4,64,128]{2,1,0:T(8,128)S(1)} %broadcast_multiply_fusion.8), channel_id=1, source_target_pairs={{0,1},{1,2},{2,3},{3,4},{4,5},{5,6},{6,7},{7,8},{8,9},{9,10},{10,1... | collective-permute-start | bytes 393224 | tf_op jit(solution)/shard_map/ppermute | solution.py:12
  82.6 56.8 %collective-permute-start.18 = (f32[4,64,128]{2,1,0:T(8,128)S(1)}, f32[4,64,128]{2,1,0:T(8,128)S(1)}, u32[]{:S(2)}, u32[]{:S(2)}) collective-permute-start(f32[4,64,128]{2,1,0:T(8,128)S(1)} %broadcast_multiply_fusion.7), channel_id=1, source_target_pairs={{0,32},{1,33},{2,34},{3,35},{4,36},{5,37},{6,38},{7,39},{8,40},{9,... | collective-permute-start | bytes 393224 | tf_op jit(solution)/shard_map/ppermute | solution.py:12
  82.7 59.7 %collective-permute-start.16 = (f32[4,64,128]{2,1,0:T(8,128)S(1)}, f32[4,64,128]{2,1,0:T(8,128)S(1)}, u32[]{:S(2)}, u32[]{:S(2)}) collective-permute-start(f32[4,64,128]{2,1,0:T(8,128)S(1)} %broadcast_multiply_fusion.9), channel_id=1, source_target_pairs={{0,224},{1,225},{2,226},{3,227},{4,228},{5,229},{6,230},{7,231},{8... | collective-permute-start | bytes 393224 | tf_op jit(solution)/shard_map/ppermute | solution.py:12
  109.2 6.0 %collective-permute-start.15 = (bf16[4,128]{1,0:T(4,128)(2,1)}, bf16[4,128]{1,0:T(4,128)(2,1)}, u32[]{:S(2)}, u32[]{:S(2)}) collective-permute-start(bf16[4,128]{1,0:T(4,128)(2,1)} %pad_maximum_fusion.5), channel_id=1, source_target_pairs={{0,225},{1,226},{2,227},{3,228},{4,229},{5,230},{6,231},{7,232},{8... | collective-permute-start | bytes 3080 | tf_op jit(solution)/shard_map/ppermute | solution.py:12
  109.3 1.7 copy-start.15
  111.0 2.3 copy-start.14
  113.3 40.6 %copy-start.31 = (f32[4,128]{1,0:T(4,128)S(1)}, f32[4,128]{1,0:T(4,128)}, u32[]{:S(2)}) copy-start(f32[4,128]{1,0:T(4,128)} %add_add_fusion.3) | copy-start | bytes 6148
  115.2 3.7 collective-permute-start.14
  118.9 5.4 %collective-permute-start.13 = (bf16[4,128]{1,0:T(4,128)(2,1)}, bf16[4,128]{1,0:T(4,128)(2,1)S(1)}, u32[]{:S(2)}, u32[]{:S(2)}) collective-permute-start(bf16[4,128]{1,0:T(4,128)(2,1)} %pad_maximum_fusion.5), channel_id=1, source_target_pairs={{0,31},{1,32},{2,33},{3,34},{4,35},{5,36},{6,37},{7,38},{8,39},{9,... | collective-permute-start | bytes 3080 | tf_op jit(solution)/shard_map/ppermute | solution.py:12
  124.3 7.9 %collective-permute-start.12 = (bf16[4,128]{1,0:T(4,128)(2,1)}, bf16[4,128]{1,0:T(4,128)(2,1)S(1)}, u32[]{:S(2)}, u32[]{:S(2)}) collective-permute-start(bf16[4,128]{1,0:T(4,128)(2,1)} %pad_maximum_fusion.5), channel_id=1, source_target_pairs={{0,33},{1,34},{2,35},{3,36},{4,37},{5,38},{6,39},{7,40},{8,41},{9,... | collective-permute-start | bytes 3080 | tf_op jit(solution)/shard_map/ppermute | solution.py:12
  132.1 61.4 %collective-permute-start.11 = (bf16[4,64,128]{2,1,0:T(8,128)(2,1)S(1)}, bf16[4,64,128]{2,1,0:T(8,128)(2,1)S(1)}, u32[]{:S(2)}, u32[]{:S(2)}) collective-permute-start(bf16[4,64,128]{2,1,0:T(8,128)(2,1)S(1)} %pad_maximum_fusion.3), channel_id=1, source_target_pairs={{0,1},{1,2},{2,3},{3,4},{4,5},{5,6},{6,7},{7,8},{8,9},{9,10},{10,1... | collective-permute-start | bytes 196616 | tf_op jit(solution)/shard_map/ppermute | solution.py:12
  133.9 55.6 %collective-permute-start.10 = (bf16[4,64,128]{2,1,0:T(8,128)(2,1)S(1)}, bf16[4,64,128]{2,1,0:T(8,128)(2,1)S(1)}, u32[]{:S(2)}, u32[]{:S(2)}) collective-permute-start(bf16[4,64,128]{2,1,0:T(8,128)(2,1)S(1)} %pad_maximum_fusion.3), channel_id=1, source_target_pairs={{0,224},{1,225},{2,226},{3,227},{4,228},{5,229},{6,230},{7,231},{8... | collective-permute-start | bytes 196616 | tf_op jit(solution)/shard_map/ppermute | solution.py:12
  135.6 58.0 %collective-permute-start.9 = (bf16[4,64,128]{2,1,0:T(8,128)(2,1)S(1)}, bf16[4,64,128]{2,1,0:T(8,128)(2,1)S(1)}, u32[]{:S(2)}, u32[]{:S(2)}) collective-permute-start(bf16[4,64,128]{2,1,0:T(8,128)(2,1)S(1)} %pad_maximum_fusion.3), channel_id=1, source_target_pairs={{0,255},{1,0},{2,1},{3,2},{4,3},{5,4},{6,5},{7,6},{8,7},{9,8},{10,... | collective-permute-start | bytes 196616 | tf_op jit(solution)/shard_map/ppermute | solution.py:12
  139.4 54.2 %collective-permute-start.8 = (bf16[4,64,128]{2,1,0:T(8,128)(2,1)S(1)}, bf16[4,64,128]{2,1,0:T(8,128)(2,1)S(1)}, u32[]{:S(2)}, u32[]{:S(2)}) collective-permute-start(bf16[4,64,128]{2,1,0:T(8,128)(2,1)S(1)} %pad_maximum_fusion.3), channel_id=1, source_target_pairs={{0,32},{1,33},{2,34},{3,35},{4,36},{5,37},{6,38},{7,39},{8,40},{9,... | collective-permute-start | bytes 196616 | tf_op jit(solution)/shard_map/ppermute | solution.py:12
  161.0 3.7 copy-start.5
  188.0 1.4 copy-start.4
  203.0 1.8 copy-start.39
  203.0 1.8 copy-start.37
  203.0 1.9 copy-start.35
  203.0 2.0 copy-start.33
  205.1 38.1 %collective-permute-start.31 = (f32[4,128]{1,0:T(4,128)S(1)}, f32[4,128]{1,0:T(4,128)S(1)}, u32[]{:S(2)}, u32[]{:S(2)}) collective-permute-start(f32[4,128]{1,0:T(4,128)S(1)} %broadcast_multiply_fusion.10), channel_id=1, source_target_pairs={{0,31},{1,32},{2,33},{3,34},{4,35},{5,36},{6,37},{7,38},{8,39},{9,... | collective-permute-start | bytes 6152 | tf_op jit(solution)/shard_map/ppermute | solution.py:12
  209.9 34.6 %collective-permute-start.30 = (f32[4,128]{1,0:T(4,128)S(1)}, f32[4,128]{1,0:T(4,128)S(1)}, u32[]{:S(2)}, u32[]{:S(2)}) collective-permute-start(f32[4,128]{1,0:T(4,128)S(1)} %broadcast_multiply_fusion.11), channel_id=1, source_target_pairs={{0,33},{1,34},{2,35},{3,36},{4,37},{5,38},{6,39},{7,40},{8,41},{9,... | collective-permute-start | bytes 6152 | tf_op jit(solution)/shard_map/ppermute | solution.py:12
  209.9 40.7 %collective-permute-start.28 = (f32[4,128]{1,0:T(4,128)S(1)}, f32[4,128]{1,0:T(4,128)S(1)}, u32[]{:S(2)}, u32[]{:S(2)}) collective-permute-start(f32[4,128]{1,0:T(4,128)S(1)} %broadcast_multiply_fusion.13), channel_id=1, source_target_pairs={{0,223},{1,224},{2,225},{3,226},{4,227},{5,228},{6,229},{7,230},{8... | collective-permute-start | bytes 6152 | tf_op jit(solution)/shard_map/ppermute | solution.py:12
  214.1 36.6 %collective-permute-start.29 = (f32[4,128]{1,0:T(4,128)S(1)}, f32[4,128]{1,0:T(4,128)S(1)}, u32[]{:S(2)}, u32[]{:S(2)}) collective-permute-start(f32[4,128]{1,0:T(4,128)S(1)} %broadcast_multiply_fusion.12), channel_id=1, source_target_pairs={{0,225},{1,226},{2,227},{3,228},{4,229},{5,230},{6,231},{7,232},{8... | collective-permute-start | bytes 6152 | tf_op jit(solution)/shard_map/ppermute | solution.py:12
  216.3 3.8 copy-start.30
  216.3 9.8 %copy-start.13 = (bf16[1,64,64,128]{3,1,2,0:T(8,128)(2,1)S(1)}, bf16[1,64,64,128]{3,1,2,0:T(8,128)(2,1)}, u32[]{:S(2)}) copy-start(bf16[1,64,64,128]{3,1,2,0:T(8,128)(2,1)} %get-tuple-element.426) | copy-start | bytes 3145732
  219.2 7.6 %copy-start.12 = (bf16[1,64,64,128]{3,1,2,0:T(8,128)(2,1)S(1)}, bf16[1,64,64,128]{3,1,2,0:T(8,128)(2,1)}, u32[]{:S(2)}) copy-start(bf16[1,64,64,128]{3,1,2,0:T(8,128)(2,1)} %get-tuple-element.427) | copy-start | bytes 3145732
  221.6 29.1 %collective-permute-start.26 = (f32[4,64,128]{2,1,0:T(8,128)}, f32[4,64,128]{2,1,0:T(8,128)}, u32[]{:S(2)}, u32[]{:S(2)}) collective-permute-start(f32[4,64,128]{2,1,0:T(8,128)} %broadcast_multiply_fusion.3), channel_id=1, source_target_pairs={{0,32},{1,33},{2,34},{3,35},{4,36},{5,37},{6,38},{7,39},{8,40},{9,... | collective-permute-start | bytes 393224 | tf_op jit(solution)/shard_map/ppermute | solution.py:12
  226.1 1.4 copy-start.2
  239.9 1.3 copy-start.20
  240.0 1.3 copy-start.21
  240.0 1.3 copy-start.22
  240.0 1.3 copy-start.23
  240.0 1.3 copy-start.24
  241.3 1.9 copy-start.19
  241.4 3.2 copy-start.18
  241.4 9.3 %copy-start.17 = (f32[4,64,128]{2,1,0:T(8,128)S(1)}, f32[4,64,128]{2,1,0:T(8,128)}, u32[]{:S(2)}) copy-start(f32[4,64,128]{2,1,0:T(8,128)} %broadcast_multiply_fusion.4) | copy-start | bytes 393220
  243.2 7.5 %collective-permute-start.24 = (f32[4,64,128]{2,1,0:T(8,128)S(1)}, f32[4,64,128]{2,1,0:T(8,128)S(1)}, u32[]{:S(2)}, u32[]{:S(2)}) collective-permute-start(f32[4,64,128]{2,1,0:T(8,128)S(1)} %copy-done.19), channel_id=1, source_target_pairs={{0,224},{1,225},{2,226},{3,227},{4,228},{5,229},{6,230},{7,231},{8... | collective-permute-start | bytes 393224 | tf_op jit(solution)/shard_map/ppermute | solution.py:12
  244.6 8.6 %collective-permute-start.27 = (f32[4,64,128]{2,1,0:T(8,128)S(1)}, f32[4,64,128]{2,1,0:T(8,128)S(1)}, u32[]{:S(2)}, u32[]{:S(2)}) collective-permute-start(f32[4,64,128]{2,1,0:T(8,128)S(1)} %copy-done.18), channel_id=1, source_target_pairs={{0,255},{1,0},{2,1},{3,2},{4,3},{5,4},{6,5},{7,6},{8,7},{9,8},{10,... | collective-permute-start | bytes 393224 | tf_op jit(solution)/shard_map/ppermute | solution.py:12
  250.6 5.0 collective-permute-start.25
  260.3 249.6 %copy-start.1 = (bf16[3,3,128,128]{3,2,1,0:T(8,128)(2,1)S(1)}, bf16[3,3,128,128]{3,2,1,0:T(8,128)(2,1)}, u32[]{:S(2)}) copy-start(bf16[3,3,128,128]{3,2,1,0:T(8,128)(2,1)} %param.71) | copy-start | bytes 884740
  (17 other events, 18.9 us)
Sparse Core Ops, SparseCore 0:
  243.3 262.6 all-reduce.4
where the time goes:
time: 523 us; the launch traced here: 517 us
  waiting for transfers between devices  261 us (50%)
  starting transfers between devices  76.6 us (15%)
  local copies, waits for them, and re-layouts  75.6 us (14%)
  matrix products  36.5 us (7%)
  other arithmetic  33.6 us (6%)
  between operations  33.5 us (6%)
    psum x1, waiting for transfers between devices, local(): grad_one, grad_two = lax.psum((grad_one, grad_two), ('face', 'sub'))  244 us
    ppermute x32, starting transfers between devices, shifted(): return lax.ppermute(x, axis, [(i, (i + by) % size) for i in range(size)])  76.6 us
    dot_general x18, matrix products, conv_kernel(): lax.dot_general(window, flat_up, (((0,), (0,)), ((), ())), preferred_elem...  22.3 us
    unnamed x104, local copies, waits for them, and re-layouts  20.4 us
    ppermute x32, waiting for transfers between devices, shifted(): return lax.ppermute(x, axis, [(i, (i + by) % size) for i in range(size)])  17.3 us
  transfers between devices with their start and end apart: 33, of which 7 were waited for; matrix products, arithmetic and copies ran while one was open for 24% of the time, Pallas kernels for 0%

commit v1 on v0

--- a/solution.py
+++ b/solution.py
@@ -160,7 +160,7 @@
     grad_fields = return_halo(conv_inputs(grad_pre, kernel_one), edge_codes, corner_codes).astype(
         jnp.bfloat16
     )
-    grad_one, grad_two = lax.psum((grad_one, grad_two), ("face", "sub"))
+    grad_one, grad_two = lax.psum(lax.psum((grad_one, grad_two), "face"), "sub")
     return (outputs[None], grad_fields[None], grad_one * norm_factor, grad_two * norm_factor)
 
 

time: 523 us -> 1510 us (2.89)
  waiting for transfers between devices: 261 us -> 1250 us
    psum x1 -> x2, waiting for transfers between devices: 244 us -> 1230 us  [local(): grad_one, grad_two = lax.psum(lax.psum((grad_one, grad_two), 'face'), 'sub')]
  transfers between devices with their start and end apart: 33 -> 34, of which waited for: 7 -> 8; matrix products, arithmetic and copies ran while one was open for 24% -> 8% of each run, Pallas kernels for 0% -> 0%
where the time goes in v1:
time: 1510 us; the launch traced here: 1500 us
  waiting for transfers between devices  1250 us (83%)
  starting transfers between devices  76.7 us (5%)
  local copies, waits for them, and re-layouts  75.7 us (5%)
  matrix products  36.6 us (2%)
  between operations  34 us (2%)
  other arithmetic  33.8 us (2%)
    psum x2, waiting for transfers between devices, local(): grad_one, grad_two = lax.psum(lax.psum((grad_one, grad_two), 'face'), 'sub')  1230 us
    ppermute x32, starting transfers between devices, shifted(): return lax.ppermute(x, axis, [(i, (i + by) % size) for i in range(size)])  76.6 us
  transfers between devices with their start and end apart: 34, of which 8 were waited for; matrix products, arithmetic and copies ran while one was open for 8% of the time, Pallas kernels for 0%

profile of v1, /device:TPU:8, one launch (start us, length us, event | category | flops | bytes accessed | tf_op | source)
XLA Modules:
  0.0 1504.5 jit_solution(3917661871559977100)
XLA Ops:
  8.0 3.3 collective-permute-start.7
  12.3 5.7 collective-permute-start.5
  33.2 1.9 copy.179
  36.2 3.1 convolution_select_fusion.1
  45.0 2.0 and_reduce_fusion
  52.1 1.7 slice.1266
  53.8 1.5 pad.122
  57.9 4.2 collective-permute-start.20
  62.2 4.5 collective-permute-start.23
  66.9 3.7 collective-permute-start.2
  70.5 4.6 collective-permute-start.1
  75.5 4.6 collective-permute-start.19
  80.8 2.3 collective-permute-done
  83.2 5.7 collective-permute-start.16
  90.4 1.4 scatter.54
  91.8 1.7 scatter.55
  93.5 1.4 scatter.56
  94.9 1.7 scatter.59
  101.6 1.4 copy.155
  103.8 5.0 add_divide_fusion
  111.6 1.8 copy.116
  113.9 1.9 copy.117
  115.8 2.2 collective-permute-start.14
  119.5 3.8 collective-permute-start.13
  123.4 1.5 collective-permute-done.13
  125.1 7.6 collective-permute-done.12
  132.7 1.9 collective-permute-start.11
  134.6 1.7 collective-permute-start.10
  136.3 3.6 collective-permute-start.9
  140.0 3.0 collective-permute-start.8
  144.1 1.8 scatter-add.54
  145.8 2.6 fusion.45
  148.5 2.3 broadcast_select_fusion.1
  150.8 2.4 scatter-add.56
  161.7 3.7 fusion.5
  165.3 2.0 convolution_bitcast_fusion.16
  167.3 2.0 convolution_bitcast_fusion.15
  169.3 1.9 convolution_bitcast_fusion.14
  171.2 2.0 convolution_bitcast_fusion.13
  173.2 2.0 convolution_bitcast_fusion.12
  175.2 1.9 convolution_bitcast_fusion.11
  177.1 2.0 convolution_bitcast_fusion.10
  179.1 2.0 convolution_bitcast_fusion.9
  181.1 2.3 convolution_bitcast_fusion.17
  184.4 3.1 convolution_select_fusion
  188.8 1.3 copy-done.4
  190.9 3.3 slice.1289
  195.5 3.9 fusion.71
  200.5 2.9 select_convert_fusion
  203.9 1.6 copy.147
  205.8 4.8 collective-permute-start.31
  210.6 4.1 collective-permute-start.28
  217.0 2.9 copy.152
  222.3 4.5 collective-permute-start.26
  244.0 1.4 collective-permute-start.24
  245.3 6.0 collective-permute-start.27
  251.4 2.5 collective-permute-done.27
  253.9 2.5 collective-permute-done.25
  258.8 1.4 broadcast_select_fusion
  261.0 1180.9 %all-reduce.7.cloned.1.call-done = (f32[3,3,128,128]{3,2,1,0:T(8,128)}, f32[3,3,128,128]{3,2,1,0:T(8,128)}) async-done(((f32[3,3,128,128]{3,2,1,0:T(8,128)}, f32[3,3,128,128]{3,2,1,0:T(8,128)}), (f32[3,3,128,128]{3,2,1,0:T(8,128)}, f32[3,3,128,128]{3,2,1,0:T(8,128)})) %all-reduce.7.cloned.1.call-update) | async-done | bytes 1179664 | tf_op jit(solution)/shard_map/psum | solution.py:163
  1442.4 1.6 copy.148
  1444.0 49.5 %all-reduce.9.cloned.1.call-done = (f32[3,3,128,128]{3,2,1,0:T(8,128)}, f32[3,3,128,128]{3,2,1,0:T(8,128)}) async-done(((f32[3,3,128,128]{3,2,1,0:T(8,128)}, f32[3,3,128,128]{3,2,1,0:T(8,128)}), (f32[3,3,128,128]{3,2,1,0:T(8,128)}, f32[3,3,128,128]{3,2,1,0:T(8,128)})) %all-reduce.9.cloned.1.call-update) | async-done | bytes 1179664 | tf_op jit(solution)/shard_map/psum | solution.py:163
  1493.5 1.9 broadcast_multiply_fusion.1
  1495.4 1.9 broadcast_multiply_fusion
  (333 shorter events, 66.9 us)
Async XLA Ops:
  7.2 96.2 %copy-start = (bf16[3,3,128,128]{3,2,1,0:T(8,128)(2,1)S(1)}, bf16[3,3,128,128]{3,2,1,0:T(8,128)(2,1)}, u32[]{:S(2)}) copy-start(bf16[3,3,128,128]{3,2,1,0:T(8,128)(2,1)} %param.71) | copy-start | bytes 884740
  7.2 1434.7 %all-reduce.7.cloned.1.call-start = ((), (), s32[]{:S(2)}) async-start(), calls=%async_computation | async-start | bytes 2359296 | tf_op jit(solution)/shard_map/psum | solution.py:163
  8.0 49.9 %collective-permute-start.7 = (bf16[4,128]{1,0:T(4,128)(2,1)S(1)}, bf16[4,128]{1,0:T(4,128)(2,1)S(1)}, u32[]{:S(2)}, u32[]{:S(2)}) collective-permute-start(bf16[4,128]{1,0:T(4,128)(2,1)S(1)} %pad_maximum_fusion.4), channel_id=1, source_target_pairs={{0,225},{1,226},{2,227},{3,228},{4,229},{5,230},{6,231},{7,232},{8... | collective-permute-start | bytes 3080 | tf_op jit(solution)/shard_map/ppermute | solution.py:12
  11.3 50.8 %collective-permute-start.6 = (bf16[4,128]{1,0:T(4,128)(2,1)S(1)}, bf16[4,128]{1,0:T(4,128)(2,1)S(1)}, u32[]{:S(2)}, u32[]{:S(2)}) collective-permute-start(bf16[4,128]{1,0:T(4,128)(2,1)S(1)} %pad_maximum_fusion.4), channel_id=1, source_target_pairs={{0,223},{1,224},{2,225},{3,226},{4,227},{5,228},{6,229},{7,230},{8... | collective-permute-start | bytes 3080 | tf_op jit(solution)/shard_map/ppermute | solution.py:12
  12.3 49.9 %collective-permute-start.5 = (bf16[4,128]{1,0:T(4,128)(2,1)S(1)}, bf16[4,128]{1,0:T(4,128)(2,1)S(1)}, u32[]{:S(2)}, u32[]{:S(2)}) collective-permute-start(bf16[4,128]{1,0:T(4,128)(2,1)S(1)} %pad_maximum_fusion.4), channel_id=1, source_target_pairs={{0,31},{1,32},{2,33},{3,34},{4,35},{5,36},{6,37},{7,38},{8,39},{9,... | collective-permute-start | bytes 3080 | tf_op jit(solution)/shard_map/ppermute | solution.py:12
  18.0 48.7 %collective-permute-start.4 = (bf16[4,128]{1,0:T(4,128)(2,1)S(1)}, bf16[4,128]{1,0:T(4,128)(2,1)S(1)}, u32[]{:S(2)}, u32[]{:S(2)}) collective-permute-start(bf16[4,128]{1,0:T(4,128)(2,1)S(1)} %pad_maximum_fusion.4), channel_id=1, source_target_pairs={{0,33},{1,34},{2,35},{3,36},{4,37},{5,38},{6,39},{7,40},{8,41},{9,... | collective-permute-start | bytes 3080 | tf_op jit(solution)/shard_map/ppermute | solution.py:12
  19.8 69.1 %collective-permute-start.3 = (bf16[4,64,128]{2,1,0:T(8,128)(2,1)S(1)}, bf16[4,64,128]{2,1,0:T(8,128)(2,1)}, u32[]{:S(2)}, u32[]{:S(2)}) collective-permute-start(bf16[4,64,128]{2,1,0:T(8,128)(2,1)S(1)} %pad_maximum_fusion.2), channel_id=1, source_target_pairs={{0,1},{1,2},{2,3},{3,4},{4,5},{5,6},{6,7},{7,8},{8,9},{9,10},{10,1... | collective-permute-start | bytes 196616 | tf_op jit(solution)/shard_map/ppermute | solution.py:12
  39.9 5.1 copy-start.40
  39.9 5.1 copy-start.41
  40.1 13.8 copy-start.3
  41.6 2.2 copy-start.32
  41.6 12.2 copy-start.29
  42.3 1.6 copy-start.34
  43.6 10.2 copy-start.36
  52.1 1.7 copy-start.16
  57.9 9.0 collective-permute-start.20
  62.1 8.4 collective-permute-start.22
  62.2 12.9 collective-permute-start.23
  66.7 8.8 collective-permute-start.21
  66.9 16.3 %collective-permute-start.2 = (bf16[4,64,128]{2,1,0:T(8,128)(2,1)S(1)}, bf16[4,64,128]{2,1,0:T(8,128)(2,1)S(1)}, u32[]{:S(2)}, u32[]{:S(2)}) collective-permute-start(bf16[4,64,128]{2,1,0:T(8,128)(2,1)S(1)} %pad_maximum_fusion.2), channel_id=1, source_target_pairs={{0,224},{1,225},{2,226},{3,227},{4,228},{5,229},{6,230},{7,231},{8... | collective-permute-start | bytes 196616 | tf_op jit(solution)/shard_map/ppermute | solution.py:12
  70.5 10.2 collective-permute-start.1
  75.1 8.0 collective-permute-start
  75.5 59.1 %collective-permute-start.19 = (f32[4,64,128]{2,1,0:T(8,128)}, f32[4,64,128]{2,1,0:T(8,128)S(1)}, u32[]{:S(2)}, u32[]{:S(2)}) collective-permute-start(f32[4,64,128]{2,1,0:T(8,128)} %broadcast_multiply_fusion.6), channel_id=1, source_target_pairs={{0,255},{1,0},{2,1},{3,2},{4,3},{5,4},{6,5},{7,6},{8,7},{9,8},{10,... | collective-permute-start | bytes 393224 | tf_op jit(solution)/shard_map/ppermute | solution.py:12
  80.7 55.6 %collective-permute-start.17 = (f32[4,64,128]{2,1,0:T(8,128)S(1)}, f32[4,64,128]{2,1,0:T(8,128)S(1)}, u32[]{:S(2)}, u32[]{:S(2)}) collective-permute-start(f32[4,64,128]{2,1,0:T(8,128)S(1)} %broadcast_multiply_fusion.8), channel_id=1, source_target_pairs={{0,1},{1,2},{2,3},{3,4},{4,5},{5,6},{6,7},{7,8},{8,9},{9,10},{10,1... | collective-permute-start | bytes 393224 | tf_op jit(solution)/shard_map/ppermute | solution.py:12
  83.1 56.9 %collective-permute-start.18 = (f32[4,64,128]{2,1,0:T(8,128)S(1)}, f32[4,64,128]{2,1,0:T(8,128)S(1)}, u32[]{:S(2)}, u32[]{:S(2)}) collective-permute-start(f32[4,64,128]{2,1,0:T(8,128)S(1)} %broadcast_multiply_fusion.7), channel_id=1, source_target_pairs={{0,32},{1,33},{2,34},{3,35},{4,36},{5,37},{6,38},{7,39},{8,40},{9,... | collective-permute-start | bytes 393224 | tf_op jit(solution)/shard_map/ppermute | solution.py:12
  83.2 59.9 %collective-permute-start.16 = (f32[4,64,128]{2,1,0:T(8,128)S(1)}, f32[4,64,128]{2,1,0:T(8,128)S(1)}, u32[]{:S(2)}, u32[]{:S(2)}) collective-permute-start(f32[4,64,128]{2,1,0:T(8,128)S(1)} %broadcast_multiply_fusion.9), channel_id=1, source_target_pairs={{0,224},{1,225},{2,226},{3,227},{4,228},{5,229},{6,230},{7,231},{8... | collective-permute-start | bytes 393224 | tf_op jit(solution)/shard_map/ppermute | solution.py:12
  109.8 6.0 collective-permute-start.15
  109.9 1.7 copy-start.15
  111.5 2.3 copy-start.14
  113.9 40.7 %copy-start.31 = (f32[4,128]{1,0:T(4,128)S(1)}, f32[4,128]{1,0:T(4,128)}, u32[]{:S(2)}) copy-start(f32[4,128]{1,0:T(4,128)} %add_add_fusion.3) | copy-start | bytes 6148
  115.8 3.7 collective-permute-start.14
  119.5 5.4 collective-permute-start.13
  124.9 7.9 collective-permute-start.12
  132.7 61.5 %collective-permute-start.11 = (bf16[4,64,128]{2,1,0:T(8,128)(2,1)S(1)}, bf16[4,64,128]{2,1,0:T(8,128)(2,1)S(1)}, u32[]{:S(2)}, u32[]{:S(2)}) collective-permute-start(bf16[4,64,128]{2,1,0:T(8,128)(2,1)S(1)} %pad_maximum_fusion.3), channel_id=1, source_target_pairs={{0,1},{1,2},{2,3},{3,4},{4,5},{5,6},{6,7},{7,8},{8,9},{9,10},{10,1... | collective-permute-start | bytes 196616 | tf_op jit(solution)/shard_map/ppermute | solution.py:12
  134.6 55.5 %collective-permute-start.10 = (bf16[4,64,128]{2,1,0:T(8,128)(2,1)S(1)}, bf16[4,64,128]{2,1,0:T(8,128)(2,1)S(1)}, u32[]{:S(2)}, u32[]{:S(2)}) collective-permute-start(bf16[4,64,128]{2,1,0:T(8,128)(2,1)S(1)} %pad_maximum_fusion.3), channel_id=1, source_target_pairs={{0,224},{1,225},{2,226},{3,227},{4,228},{5,229},{6,230},{7,231},{8... | collective-permute-start | bytes 196616 | tf_op jit(solution)/shard_map/ppermute | solution.py:12
  136.3 58.0 %collective-permute-start.9 = (bf16[4,64,128]{2,1,0:T(8,128)(2,1)S(1)}, bf16[4,64,128]{2,1,0:T(8,128)(2,1)S(1)}, u32[]{:S(2)}, u32[]{:S(2)}) collective-permute-start(bf16[4,64,128]{2,1,0:T(8,128)(2,1)S(1)} %pad_maximum_fusion.3), channel_id=1, source_target_pairs={{0,255},{1,0},{2,1},{3,2},{4,3},{5,4},{6,5},{7,6},{8,7},{9,8},{10,... | collective-permute-start | bytes 196616 | tf_op jit(solution)/shard_map/ppermute | solution.py:12
  140.0 54.4 %collective-permute-start.8 = (bf16[4,64,128]{2,1,0:T(8,128)(2,1)S(1)}, bf16[4,64,128]{2,1,0:T(8,128)(2,1)S(1)}, u32[]{:S(2)}, u32[]{:S(2)}) collective-permute-start(bf16[4,64,128]{2,1,0:T(8,128)(2,1)S(1)} %pad_maximum_fusion.3), channel_id=1, source_target_pairs={{0,32},{1,33},{2,34},{3,35},{4,36},{5,37},{6,38},{7,39},{8,40},{9,... | collective-permute-start | bytes 196616 | tf_op jit(solution)/shard_map/ppermute | solution.py:12
  161.7 3.7 copy-start.5
  188.7 1.4 copy-start.4
  203.7 1.8 copy-start.39
  203.7 1.8 copy-start.37
  203.8 1.9 copy-start.35
  203.8 2.0 copy-start.33
  205.8 38.1 %collective-permute-start.31 = (f32[4,128]{1,0:T(4,128)S(1)}, f32[4,128]{1,0:T(4,128)S(1)}, u32[]{:S(2)}, u32[]{:S(2)}) collective-permute-start(f32[4,128]{1,0:T(4,128)S(1)} %broadcast_multiply_fusion.10), channel_id=1, source_target_pairs={{0,31},{1,32},{2,33},{3,34},{4,35},{5,36},{6,37},{7,38},{8,39},{9,... | collective-permute-start | bytes 6152 | tf_op jit(solution)/shard_map/ppermute | solution.py:12
  210.6 34.7 %collective-permute-start.30 = (f32[4,128]{1,0:T(4,128)S(1)}, f32[4,128]{1,0:T(4,128)S(1)}, u32[]{:S(2)}, u32[]{:S(2)}) collective-permute-start(f32[4,128]{1,0:T(4,128)S(1)} %broadcast_multiply_fusion.11), channel_id=1, source_target_pairs={{0,33},{1,34},{2,35},{3,36},{4,37},{5,38},{6,39},{7,40},{8,41},{9,... | collective-permute-start | bytes 6152 | tf_op jit(solution)/shard_map/ppermute | solution.py:12
  210.6 40.7 %collective-permute-start.28 = (f32[4,128]{1,0:T(4,128)S(1)}, f32[4,128]{1,0:T(4,128)S(1)}, u32[]{:S(2)}, u32[]{:S(2)}) collective-permute-start(f32[4,128]{1,0:T(4,128)S(1)} %broadcast_multiply_fusion.13), channel_id=1, source_target_pairs={{0,223},{1,224},{2,225},{3,226},{4,227},{5,228},{6,229},{7,230},{8... | collective-permute-start | bytes 6152 | tf_op jit(solution)/shard_map/ppermute | solution.py:12
  214.8 36.6 %collective-permute-start.29 = (f32[4,128]{1,0:T(4,128)S(1)}, f32[4,128]{1,0:T(4,128)S(1)}, u32[]{:S(2)}, u32[]{:S(2)}) collective-permute-start(f32[4,128]{1,0:T(4,128)S(1)} %broadcast_multiply_fusion.12), channel_id=1, source_target_pairs={{0,225},{1,226},{2,227},{3,228},{4,229},{5,230},{6,231},{7,232},{8... | collective-permute-start | bytes 6152 | tf_op jit(solution)/shard_map/ppermute | solution.py:12
  217.0 3.8 copy-start.30
  217.0 9.8 copy-start.13
  219.9 7.6 copy-start.12
  222.3 29.1 %collective-permute-start.26 = (f32[4,64,128]{2,1,0:T(8,128)}, f32[4,64,128]{2,1,0:T(8,128)}, u32[]{:S(2)}, u32[]{:S(2)}) collective-permute-start(f32[4,64,128]{2,1,0:T(8,128)} %broadcast_multiply_fusion.3), channel_id=1, source_target_pairs={{0,32},{1,33},{2,34},{3,35},{4,36},{5,37},{6,38},{7,39},{8,40},{9,... | collective-permute-start | bytes 393224 | tf_op jit(solution)/shard_map/ppermute | solution.py:12
  226.8 1.4 copy-start.2
  240.6 1.3 copy-start.20
  240.7 1.3 copy-start.22
  240.7 1.3 copy-start.23
  240.7 1.3 copy-start.24
  242.0 1.9 copy-start.19
  242.1 3.3 copy-start.18
  242.1 9.3 copy-start.17
  243.9 1249.6 %all-reduce.9.cloned.1.call-start = ((), (), s32[]{:S(2)}) async-start(), calls=%async_computation.1 | async-start | bytes 2359296 | tf_op jit(solution)/shard_map/psum | solution.py:163
  244.0 7.5 collective-permute-start.24
  245.3 8.6 collective-permute-start.27
  251.4 5.0 collective-permute-start.25
  1442.1 55.2 %copy-start.1 = (bf16[3,3,128,128]{3,2,1,0:T(8,128)(2,1)S(1)}, bf16[3,3,128,128]{3,2,1,0:T(8,128)(2,1)}, u32[]{:S(2)}) copy-start(bf16[3,3,128,128]{3,2,1,0:T(8,128)(2,1)} %param.71) | copy-start | bytes 884740
  (18 other events, 20.2 us)
Sparse Core Ops, SparseCore 0:
  244.0 1197.8 all-reduce.6
  1444.7 48.7 all-reduce.8
